TPU v7x, 32 devices: a whole 2x2x4 slice. The times are simulated.
32 devices in a mesh: ax: 16 (over z, y, x), rad: 2 (over core).
Axes of the slice: x: 2, y: 2, z: 4, core: 2. Of those that a mesh axis runs over, the one named last changes fastest.
Arguments:
- fields: float32 [128, 5, 8, 1024], P('ax', None, None, 'rad'), may hold values from -6 to 6
Outputs:
- axial_deriv: float32 [128, 5, 8, 1024], P('ax', None, None, 'rad')
- filtered: float32 [128, 5, 8, 1024], P('ax', None, None, 'rad')
- radial_deriv: float32 [128, 5, 8, 1024], P('ax', None, None, 'rad')
All inputs are finite; a program needn't handle non-finite values.
Results may differ from a plain program's by a relative error of at most 0.0003.
Values sent between devices are 32-bit elements; how exact they have to be, the bound alone decides.
A program may use at most 128 MiB of HBM per device.

v0:
```python
import jax
import jax.numpy as jnp
from jax import lax
from jax.sharding import PartitionSpec as P

deriv_alpha = 1.0 / 3.0
filter_alpha = 0.4999
block_rows = 64


def with_halo(array, sides, width):
    for axis, dim in sides:
        size, length = (lax.axis_size(axis), array.shape[dim])
        up = [(i, (i + 1) % size) for i in range(size - 1)]
        down = [(j, i) for i, j in up]
        last = lax.slice_in_dim(array, length - width, length, axis=dim)
        initial = lax.slice_in_dim(array, 0, width, axis=dim)
        before = lax.ppermute(last, axis, up)
        after = lax.ppermute(initial, axis, down)
        array = jnp.concatenate([before, array, after], axis=dim)
    return array


def filter_weights():
    return [
        (93.0 + 70.0 * filter_alpha) / 128.0,
        (7.0 + 18.0 * filter_alpha) / 16.0,
        (-7.0 + 14.0 * filter_alpha) / 32.0,
        (1.0 - 2.0 * filter_alpha) / 16.0,
        (-1.0 + 2.0 * filter_alpha) / 128.0,
    ]


def sources(padded, count):

    def shifted(k):
        return padded[4 + k : 4 + k + count]

    deriv_rhs = 7.0 / 9.0 * (shifted(1) - shifted(-1)) + 1.0 / 36.0 * (shifted(2) - shifted(-2))
    weights = filter_weights()
    filter_rhs = weights[0] * shifted(0)
    for n in range(1, 5):
        filter_rhs = filter_rhs + weights[n] / 2.0 * (shifted(n) + shifted(-n))
    return jnp.stack([deriv_rhs, filter_rhs])


def pivots(alpha, rows):
    root = (1.0 - 4.0 * alpha * alpha) ** 0.5
    big_root = (1.0 + root) / 2.0
    ratio = (1.0 - root) / (1.0 + root)
    return big_root * (1.0 - jnp.power(ratio, rows + 2.0)) / (1.0 - jnp.power(ratio, rows + 1.0))


def tables(alpha, rows):
    length = rows.shape[-1]
    piv = pivots(alpha, rows)
    before = pivots(alpha, jnp.maximum(rows - 1.0, 0.0))
    log_fwd = jnp.log(alpha / before)
    cum_fwd = jnp.cumsum(log_fwd, axis=-1)
    log_bwd = jnp.log(alpha / piv)
    cum_bwd = jnp.cumsum(log_bwd, axis=-1)
    excl_bwd = cum_bwd - log_bwd
    index = jnp.arange(length)
    parity = ((index[:, None] - index[None, :]) % 2).astype(jnp.float32)
    signs = 1.0 - 2.0 * parity
    lower = index[:, None] >= index[None, :]
    upper = index[:, None] <= index[None, :]
    diff_fwd = jnp.minimum(cum_fwd[..., :, None] - cum_fwd[..., None, :], 0.0)
    forward = jnp.where(lower, signs * jnp.exp(diff_fwd), 0.0)
    diff_bwd = jnp.minimum(excl_bwd[..., None, :] - excl_bwd[..., :, None], 0.0)
    backward = jnp.where(upper, signs * jnp.exp(diff_bwd) / piv[..., None, :], 0.0)
    sign_in = 1.0 - 2.0 * ((index + 1) % 2).astype(jnp.float32)
    gain_in = sign_in * jnp.exp(cum_fwd)
    sign_out = 1.0 - 2.0 * ((length - index) % 2).astype(jnp.float32)
    gain_out = sign_out * jnp.exp(cum_bwd[..., length - 1 :] - excl_bwd)
    return (forward, gain_in, backward, gain_out)


def combine(earlier, later):
    return (earlier[0] * later[0], later[1] + later[0] * earlier[1])


def solve(rhs, rows, chain_forward, chain_backward):
    parts = [tables(deriv_alpha, rows), tables(filter_alpha, rows)]
    forward = jnp.stack([parts[0][0], parts[1][0]])
    gain_in = jnp.stack([parts[0][1], parts[1][1]])
    backward = jnp.stack([parts[0][2], parts[1][2]])
    gain_out = jnp.stack([parts[0][3], parts[1][3]])
    local_fwd = jnp.einsum("sbkj,sbjl->sbkl", forward, rhs, precision=lax.Precision.HIGHEST)
    incoming = chain_forward(gain_in[:, :, -1:], local_fwd[:, :, -1, :])
    eliminated = local_fwd + gain_in[..., None] * incoming[:, :, None, :]
    local_bwd = jnp.einsum("sbkj,sbjl->sbkl", backward, eliminated, precision=lax.Precision.HIGHEST)
    outgoing = chain_backward(gain_out[:, :, :1], local_bwd[:, :, 0, :])
    return local_bwd + gain_out[..., None] * outgoing[:, :, None, :]


def block_chain(coeff, offset):
    inclusive = lax.associative_scan(combine, (coeff, offset), axis=1)
    return jnp.concatenate([jnp.zeros_like(offset[:, :1]), inclusive[1][:, :-1]], axis=1)


def block_forward(coeff, offset):
    return block_chain(coeff, offset)


def block_backward(coeff, offset):
    flipped = block_chain(jnp.flip(coeff, axis=1), jnp.flip(offset, axis=1))
    return jnp.flip(flipped, axis=1)


def body(fields):
    rows_dev, count, planes, radial = fields.shape
    width = count * planes * radial
    rimmed = with_halo(fields, (("rad", 3),), 3)

    def radial_cell(k):
        return rimmed[:, :, :, 3 + k : 3 + k + radial]

    radial_deriv = (
        45.0 * (radial_cell(1) - radial_cell(-1))
        - 9.0 * (radial_cell(2) - radial_cell(-2))
        + (radial_cell(3) - radial_cell(-3))
    ) / 60.0
    flat = fields.reshape(rows_dev, width)
    lines = lax.all_to_all(flat, "ax", split_axis=1, concat_axis=0, tiled=True)
    total = lines.shape[0]
    padded = jnp.pad(lines, ((4, 4), (0, 0)))
    rhs = sources(padded, total)
    blocks = total // block_rows
    rows = jnp.arange(total, dtype=jnp.float32).reshape(blocks, block_rows)
    solved = solve(rhs.reshape(2, blocks, block_rows, -1), rows, block_forward, block_backward)
    solved = solved.reshape(2, total, -1)
    result = lax.all_to_all(solved, "ax", split_axis=1, concat_axis=2, tiled=True)
    axial_deriv = result[0].reshape(fields.shape)
    filtered = result[1].reshape(fields.shape)
    return (axial_deriv, filtered, radial_deriv)


def solution(mesh):
    in_specs = (P("ax", None, None, "rad"),)
    out_specs = (P("ax", None, None, "rad"), P("ax", None, None, "rad"), P("ax", None, None, "rad"))
    return jax.shard_map(body, mesh=mesh, in_specs=in_specs, out_specs=out_specs, check_vma=False)
```

profile of v0, /device:TPU:8, one launch (start us, length us, event | category | flops | bytes accessed | tf_op | source)
XLA Modules:
  0.0 72.5 jit_solution(13071631974729192661)
XLA Ops:
  0.6 1.3 %all_to_all.25 = f32[8,16,1280]{2,1,0:T(8,128)S(1)} reshape(f32[8,5,8,512]{3,2,1,0:T(8,128)} %param.1) | data formatting | bytes 1310720 | tf_op jit(solution)/shard_map/all_to_all | solution.py:125
  1.9 1.2 %copy.11 = f32[8,16,1280]{2,0,1:T(8,128)} copy(f32[8,16,1280]{2,1,0:T(8,128)S(1)} %all_to_all.25) | data formatting | bytes 1310720 | tf_op jit(solution)/shard_map/all_to_all | solution.py:125
  3.2 7.2 %all-to-all-start = ((f32[8,16,1280]{2,0,1:T(8,128)}), f32[8,16,1280]{2,0,1:T(8,128)S(1)}, u32[]{:S(2)}, u32[]{:S(2)}) async-start(f32[8,16,1280]{2,0,1:T(8,128)} %copy.11), calls=%async_computation | async-start | bytes 1310720 | tf_op jit(solution)/shard_map/all_to_all | solution.py:125
  10.5 0.2 reduce_window_sum.36
  10.8 0.2 reduce_window_sum.29
  11.0 0.2 reduce_window_sum.28
  11.3 0.2 reduce_window_sum.27
  11.5 0.2 slice_reduce_fusion
  12.4 15.2 %all-to-all-done = f32[8,16,1280]{2,0,1:T(8,128)S(1)} async-done(((f32[8,16,1280]{2,0,1:T(8,128)}), f32[8,16,1280]{2,0,1:T(8,128)S(1)}, u32[]{:S(2)}, u32[]{:S(2)}) %all-to-all-start) | async-done | bytes 655392 | tf_op jit(solution)/shard_map/all_to_all | solution.py:125
  27.6 0.7 multiply_add_fusion.2
  28.3 1.2 %fusion = f32[2,2,64,1280]{3,2,1,0:T(8,128)S(1)} fusion(f32[1,2,64,1280]{3,2,1,0:T(8,128)S(1)} %bitcast.45, f32[1,2,64,1280]{3,2,1,0:T(8,128)S(1)} %bitcast.44, f32[1,2,64,64]{3,2,1,0:T(8,128)S(1)} %get-tuple-element.13, f32[1,2,64,64]{3,2,1,0:T(8,128)S(1)} %get-tuple-element.14), kind=kOutput, calls=%fused_computation | convolution fusion | flops 252002304 | bytes 2686976 | tf_op jit(solution)/shard_map/sbkj,sbjl->sbkl/dot_general | solution.py:89
  29.7 1.3 %fusion.4 = f32[2,2,64,1280]{3,2,1,0:T(8,128)S(1)} fusion(f32[2,2,64,1280]{3,2,1,0:T(8,128)S(1)} %fusion, f32[2,2,1280]{2,1,0:T(2,128)S(1)} %concatenate.18, f32[2,2,64]{2,1,0:T(2,128)S(1)} %pad_maximum_fusion.1, f32[1,2,64,64]{3,2,1,0:T(8,128)S(1)} %get-tuple-element.10, f32[1,2,64,64]{3,2,1,0:T(8,128)S(1)} %get-tuple-element.9), kind=kOutput, calls=%fused_computation.5 | convolution fusion | flops 252329984 | bytes 2708480 | tf_op jit(solution)/shard_map/sbkj,sbjl->sbkl/dot_general | solution.py:92
  31.2 0.3 rev.7
  31.6 2.1 %copy.12 = f32[2,128,1280]{2,0,1:T(2,128)} copy(f32[2,128,1280]{2,1,0:T(8,128)S(1)} %bitcast.42) | data formatting | bytes 2621440 | tf_op jit(solution)/shard_map/reshape | solution.py:132
  33.7 4.8 %all-to-all-start.1 = ((f32[2,128,1280]{2,0,1:T(2,128)}), f32[2,128,1280]{2,0,1:T(2,128)S(1)}, u32[]{:S(2)}, u32[]{:S(2)}) async-start(f32[2,128,1280]{2,0,1:T(2,128)} %copy.12), calls=%async_computation.1 | async-start | bytes 2621440 | tf_op jit(solution)/shard_map/all_to_all | solution.py:133
  38.6 1.3 %collective-permute-start = (f32[8,5,8,3]{3,2,1,0:T(8,128)S(1)}, f32[8,5,8,3]{3,2,1,0:T(8,128)S(1)}, u32[]{:S(2)}, u32[]{:S(2)}) collective-permute-start(f32[8,5,8,3]{3,2,1,0:T(8,128)S(1)} %get-tuple-element.5), channel_id=1, source_target_pairs={{1,0},{3,2},{5,4},{7,6},{9,8},{11,10},{13,12},{15,14},{17,16},{19,... | collective-permute-start | bytes 11528 | tf_op jit(solution)/shard_map/ppermute | solution.py:19
  39.9 3.0 %collective-permute-start.1 = (f32[8,5,8,3]{3,2,1,0:T(8,128)S(1)}, f32[8,5,8,3]{3,2,1,0:T(8,128)S(1)}, u32[]{:S(2)}, u32[]{:S(2)}) collective-permute-start(f32[8,5,8,3]{3,2,1,0:T(8,128)S(1)} %get-tuple-element.6), channel_id=1, source_target_pairs={{0,1},{2,3},{4,5},{6,7},{8,9},{10,11},{12,13},{14,15},{16,17},{18,... | collective-permute-start | bytes 11528 | tf_op jit(solution)/shard_map/ppermute | solution.py:18
  43.0 0.9 %collective-permute-done.1 = f32[8,5,8,3]{3,2,1,0:T(8,128)S(1)} collective-permute-done((f32[8,5,8,3]{3,2,1,0:T(8,128)S(1)}, f32[8,5,8,3]{3,2,1,0:T(8,128)S(1)}, u32[]{:S(2)}, u32[]{:S(2)}) %collective-permute-start.1) | collective-permute-done | bytes 3872 | tf_op jit(solution)/shard_map/ppermute | solution.py:18
  44.0 2.0 %fusion.12 = f32[8,5,8,512]{3,2,1,0:T(8,128)} fusion(f32[8,5,8,512]{3,2,1,0:T(8,128)S(1)} %copy-done, f32[8,5,8,3]{3,2,1,0:T(8,128)S(1)} %collective-permute-done.1, f32[8,5,8,515]{3,2,1,0:T(8,128)S(1)} %constant_dynamic-update-slice_fusion), kind=kLoop, calls=%fused_computation.17 | loop fusion | flops 1802240 | bytes 3280640 | tf_op jit(solution)/shard_map/div | solution.py:119
  46.0 23.0 %all-to-all-done.1 = f32[2,128,1280]{2,0,1:T(2,128)S(1)} async-done(((f32[2,128,1280]{2,0,1:T(2,128)}), f32[2,128,1280]{2,0,1:T(2,128)S(1)}, u32[]{:S(2)}, u32[]{:S(2)}) %all-to-all-start.1) | async-done | bytes 1310752 | tf_op jit(solution)/shard_map/all_to_all | solution.py:133
  69.0 1.0 %fusion.64 = (f32[1,8,16,1280]{3,0,1,2:T(1,128)S(1)}, f32[1,8,16,1280]{3,0,1,2:T(1,128)S(1)}) fusion(f32[2,8,16,1280]{3,0,1,2:T(2,128)S(1)} %bitcast.41), kind=kLoop, calls=%fused_computation.122 | loop fusion | bytes 2621440 | tf_op jit(solution)/shard_map/slice | solution.py:135
  70.0 0.2 copy.14
  70.3 1.0 %reshape_squeeze.7 = f32[8,5,8,512]{3,2,1,0:T(8,128)} reshape(f32[1,8,16,1280]{3,2,1,0:T(8,128)S(1)} %copy.14) | data formatting | bytes 1310720 | tf_op jit(solution)/shard_map/reshape;squeeze | solution.py:135
  71.5 1.0 %reshape_squeeze.6 = f32[8,5,8,512]{3,2,1,0:T(8,128)} reshape(f32[1,8,16,1280]{3,2,1,0:T(8,128)S(1)} %copy.13) | data formatting | bytes 1310720 | tf_op jit(solution)/shard_map/reshape;squeeze | solution.py:134
  (35 shorter events, 1.6 us)
Async XLA Ops:
  3.2 24.4 %all-to-all-start = ((f32[8,16,1280]{2,0,1:T(8,128)}), f32[8,16,1280]{2,0,1:T(8,128)S(1)}, u32[]{:S(2)}, u32[]{:S(2)}) async-start(f32[8,16,1280]{2,0,1:T(8,128)} %copy.11), calls=%async_computation | async-start | bytes 1310720 | tf_op jit(solution)/shard_map/all_to_all | solution.py:125
  33.7 4.8 %copy-start = (f32[8,5,8,512]{3,2,1,0:T(8,128)S(1)}, f32[8,5,8,512]{3,2,1,0:T(8,128)}, u32[]{:S(2)}) copy-start(f32[8,5,8,512]{3,2,1,0:T(8,128)} %param.1) | copy-start | bytes 1966084
  33.7 35.3 %all-to-all-start.1 = ((f32[2,128,1280]{2,0,1:T(2,128)}), f32[2,128,1280]{2,0,1:T(2,128)S(1)}, u32[]{:S(2)}, u32[]{:S(2)}) async-start(f32[2,128,1280]{2,0,1:T(2,128)} %copy.12), calls=%async_computation.1 | async-start | bytes 2621440 | tf_op jit(solution)/shard_map/all_to_all | solution.py:133
  38.6 4.4 %collective-permute-start = (f32[8,5,8,3]{3,2,1,0:T(8,128)S(1)}, f32[8,5,8,3]{3,2,1,0:T(8,128)S(1)}, u32[]{:S(2)}, u32[]{:S(2)}) collective-permute-start(f32[8,5,8,3]{3,2,1,0:T(8,128)S(1)} %get-tuple-element.5), channel_id=1, source_target_pairs={{1,0},{3,2},{5,4},{7,6},{9,8},{11,10},{13,12},{15,14},{17,16},{19,... | collective-permute-start | bytes 11528 | tf_op jit(solution)/shard_map/ppermute | solution.py:19
  39.9 4.1 %collective-permute-start.1 = (f32[8,5,8,3]{3,2,1,0:T(8,128)S(1)}, f32[8,5,8,3]{3,2,1,0:T(8,128)S(1)}, u32[]{:S(2)}, u32[]{:S(2)}) collective-permute-start(f32[8,5,8,3]{3,2,1,0:T(8,128)S(1)} %get-tuple-element.6), channel_id=1, source_target_pairs={{0,1},{2,3},{4,5},{6,7},{8,9},{10,11},{12,13},{14,15},{16,17},{18,... | collective-permute-start | bytes 11528 | tf_op jit(solution)/shard_map/ppermute | solution.py:18
where the time goes:
time: 72.9 us; the launch traced here: 72.5 us
  waiting for transfers between devices  39.2 us (54%)
  starting transfers between devices  16.3 us (22%)
  local copies, waits for them, and re-layouts  8.85 us (12%)
  other arithmetic  4.78 us (7%)
  matrix products  2.54 us (3%)
  between operations  0.86 us (1%)
    all_to_all x1, waiting for transfers between devices, body(): lax.all_to_all(solved, 'ax', split_axis=1, concat_axis=2, tiled=True)  23 us
    all_to_all x1, waiting for transfers between devices, body(): lines = lax.all_to_all(flat, 'ax', split_axis=1, concat_axis=0, tiled=True)  15.2 us
    all_to_all x1, starting transfers between devices, body(): lines = lax.all_to_all(flat, 'ax', split_axis=1, concat_axis=0, tiled=True)  7.22 us
    all_to_all x1, starting transfers between devices, body(): lax.all_to_all(solved, 'ax', split_axis=1, concat_axis=2, tiled=True)  4.77 us
    ppermute x1, starting transfers between devices, with_halo(): before = lax.ppermute(last, axis, up)  3.05 us
    all_to_all x2, local copies, waits for them, and re-layouts, body(): lines = lax.all_to_all(flat, 'ax', split_axis=1, concat_axis=0, tiled=True)  2.53 us
    reshape x1, local copies, waits for them, and re-layouts, body(): solved = solved.reshape(2, total, -1)  2.07 us
    div x1, other arithmetic, body(): (45.0 * (radial_cell(1) - radial_cell(-1)) - 9.0 * (radial_cell(2) - radi...  2.02 us
  transfers between devices with their start and end apart: 4, of which 3 were waited for; matrix products, arithmetic and copies ran while one was open for 6% of the time, Pallas kernels for 0%

commit v1 on v0

--- a/solution.py
+++ b/solution.py
@@ -6,6 +6,22 @@
 deriv_alpha = 1.0 / 3.0
 filter_alpha = 0.4999
 block_rows = 64
+
+
+def exchange_in_pairs(value, axis, split, join):
+    ways, here = (lax.axis_size(axis), lax.axis_index(axis))
+    width = value.shape[split] // ways
+    shape = list(value.shape)
+    shape[split] = width
+    height = shape[join]
+    shape[join] = height * ways
+    full = jnp.zeros(shape, value.dtype)
+    for mask in range(ways):
+        part = lax.dynamic_slice_in_dim(value, (here ^ mask) * width, width, axis=split)
+        if mask:
+            part = lax.ppermute(part, axis, [(d, d ^ mask) for d in range(ways)])
+        full = lax.dynamic_update_slice_in_dim(full, part, (here ^ mask) * height, axis=join)
+    return full
 
 
 def with_halo(array, sides, width):
@@ -122,7 +138,7 @@
         + (radial_cell(3) - radial_cell(-3))
     ) / 60.0
     flat = fields.reshape(rows_dev, width)
-    lines = lax.all_to_all(flat, "ax", split_axis=1, concat_axis=0, tiled=True)
+    lines = exchange_in_pairs(flat, "ax", 1, 0)
     total = lines.shape[0]
     padded = jnp.pad(lines, ((4, 4), (0, 0)))
     rhs = sources(padded, total)

time: 72.9 us -> 106 us (1.45); the launches traced: 72.5 us -> 105 us
  starting transfers between devices: 16.3 us -> 52.9 us
  waiting for transfers between devices: 39.2 us -> 35 us
    ppermute x0 -> x15, starting transfers between devices: none -> 41.4 us  [exchange_in_pairs(): part = lax.ppermute(part, axis, [(d, d ^ mask) for d in range(ways)])]
    ppermute x0 -> x15, waiting for transfers between devices: none -> 22.3 us  [exchange_in_pairs(): part = lax.ppermute(part, axis, [(d, d ^ mask) for d in range(ways)])]
    all_to_all x1 -> x0, waiting for transfers between devices: 15.2 us -> none  [body(): lines = lax.all_to_all(flat, 'ax', split_axis=1, concat_axis=0, tiled=True)]
    all_to_all x1, waiting for transfers between devices: 23 us -> 11.8 us  [body(): lax.all_to_all(solved, 'ax', split_axis=1, concat_axis=2, tiled=True)]
    all_to_all x1 -> x0, starting transfers between devices: 7.22 us -> none  [body(): lines = lax.all_to_all(flat, 'ax', split_axis=1, concat_axis=0, tiled=True)]
    all_to_all x2 -> x0, local copies, waits for them, and re-layouts: 2.53 us -> none  [body(): lines = lax.all_to_all(flat, 'ax', split_axis=1, concat_axis=0, tiled=True)]
    all_to_all x1, starting transfers between devices: 4.77 us -> 7.26 us  [body(): lax.all_to_all(solved, 'ax', split_axis=1, concat_axis=2, tiled=True)]
    unnamed x5 -> x6, local copies, waits for them, and re-layouts: 0.07 us -> 1.55 us
  transfers between devices with their start and end apart: 4 -> 18, of which waited for: 3 -> 13; matrix products, arithmetic and copies ran while one was open for 6% -> 4% of each run, Pallas kernels for 0% -> 0%
where the time goes in v1:
time: 106 us; the launch traced here: 105 us
  starting transfers between devices  52.9 us (50%)
  waiting for transfers between devices  35 us (33%)
  local copies, waits for them, and re-layouts  8.09 us (8%)
  other arithmetic  4.76 us (4%)
  matrix products  2.53 us (2%)
  between operations  1.24 us (1%)
    ppermute x15, starting transfers between devices, exchange_in_pairs(): part = lax.ppermute(part, axis, [(d, d ^ mask) for d in range(ways)])  41.4 us
    ppermute x15, waiting for transfers between devices, exchange_in_pairs(): part = lax.ppermute(part, axis, [(d, d ^ mask) for d in range(ways)])  22.3 us
    all_to_all x1, waiting for transfers between devices, body(): lax.all_to_all(solved, 'ax', split_axis=1, concat_axis=2, tiled=True)  11.8 us
    all_to_all x1, starting transfers between devices, body(): lax.all_to_all(solved, 'ax', split_axis=1, concat_axis=2, tiled=True)  7.26 us
    ppermute x1, starting transfers between devices, with_halo(): before = lax.ppermute(last, axis, up)  3.05 us
  transfers between devices with their start and end apart: 18, of which 13 were waited for; matrix products, arithmetic and copies ran while one was open for 4% of the time, Pallas kernels for 0%

profile of v1, /device:TPU:8, one launch (start us, length us, event | category | flops | bytes accessed | tf_op | source)
XLA Modules:
  0.0 104.5 jit_solution(16231283856792833648)
XLA Ops:
  2.4 3.5 %collective-permute-start.14 = (f32[8,1280]{1,0:T(8,128)S(1)}, f32[8,1280]{1,0:T(8,128)S(1)}, u32[]{:S(2)}, u32[]{:S(2)}) collective-permute-start(f32[8,1280]{1,0:T(8,128)S(1)} %get-tuple-element.9), channel_id=1, source_target_pairs={{0,30},{2,28},{4,26},{6,24},{8,22},{10,20},{12,18},{14,16},{16,14}... | collective-permute-start | bytes 122888 | tf_op jit(solution)/shard_map/ppermute | solution.py:22
  13.9 2.4 %collective-permute-done.1 = f32[8,1280]{1,0:T(8,128)S(1)} collective-permute-done((f32[8,1280]{1,0:T(8,128)S(1)}, f32[8,1280]{1,0:T(8,128)S(1)}, u32[]{:S(2)}, u32[]{:S(2)}) %collective-permute-start.1) | collective-permute-done | bytes 40992 | tf_op jit(solution)/shard_map/ppermute | solution.py:22
  16.4 2.5 %collective-permute-start.2 = (f32[8,1280]{1,0:T(8,128)S(1)}, f32[8,1280]{1,0:T(8,128)S(1)}, u32[]{:S(2)}, u32[]{:S(2)}) collective-permute-start(f32[8,1280]{1,0:T(8,128)S(1)} %get-tuple-element.21), channel_id=1, source_target_pairs={{0,6},{2,4},{4,2},{6,0},{8,14},{10,12},{12,10},{14,8},{16,22},{18,... | collective-permute-start | bytes 122888 | tf_op jit(solution)/shard_map/ppermute | solution.py:22
  18.8 2.4 %collective-permute-done.2 = f32[8,1280]{1,0:T(8,128)S(1)} collective-permute-done((f32[8,1280]{1,0:T(8,128)S(1)}, f32[8,1280]{1,0:T(8,128)S(1)}, u32[]{:S(2)}, u32[]{:S(2)}) %collective-permute-start.2) | collective-permute-done | bytes 40992 | tf_op jit(solution)/shard_map/ppermute | solution.py:22
  21.3 4.0 %collective-permute-start.3 = (f32[8,1280]{1,0:T(8,128)S(1)}, f32[8,1280]{1,0:T(8,128)S(1)}, u32[]{:S(2)}, u32[]{:S(2)}) collective-permute-start(f32[8,1280]{1,0:T(8,128)S(1)} %get-tuple-element.20), channel_id=1, source_target_pairs={{0,8},{2,10},{4,12},{6,14},{8,0},{10,2},{12,4},{14,6},{16,24},{18,... | collective-permute-start | bytes 122888 | tf_op jit(solution)/shard_map/ppermute | solution.py:22
  25.3 2.0 %collective-permute-done.3 = f32[8,1280]{1,0:T(8,128)S(1)} collective-permute-done((f32[8,1280]{1,0:T(8,128)S(1)}, f32[8,1280]{1,0:T(8,128)S(1)}, u32[]{:S(2)}, u32[]{:S(2)}) %collective-permute-start.3) | collective-permute-done | bytes 40992 | tf_op jit(solution)/shard_map/ppermute | solution.py:22
  27.2 3.0 %collective-permute-start.4 = (f32[8,1280]{1,0:T(8,128)S(1)}, f32[8,1280]{1,0:T(8,128)S(1)}, u32[]{:S(2)}, u32[]{:S(2)}) collective-permute-start(f32[8,1280]{1,0:T(8,128)S(1)} %get-tuple-element.19), channel_id=1, source_target_pairs={{0,10},{2,8},{4,14},{6,12},{8,2},{10,0},{12,6},{14,4},{16,26},{18,... | collective-permute-start | bytes 122888 | tf_op jit(solution)/shard_map/ppermute | solution.py:22
  30.3 2.0 %collective-permute-done.4 = f32[8,1280]{1,0:T(8,128)S(1)} collective-permute-done((f32[8,1280]{1,0:T(8,128)S(1)}, f32[8,1280]{1,0:T(8,128)S(1)}, u32[]{:S(2)}, u32[]{:S(2)}) %collective-permute-start.4) | collective-permute-done | bytes 40992 | tf_op jit(solution)/shard_map/ppermute | solution.py:22
  32.2 3.0 %collective-permute-start.5 = (f32[8,1280]{1,0:T(8,128)S(1)}, f32[8,1280]{1,0:T(8,128)S(1)}, u32[]{:S(2)}, u32[]{:S(2)}) collective-permute-start(f32[8,1280]{1,0:T(8,128)S(1)} %get-tuple-element.18), channel_id=1, source_target_pairs={{0,12},{2,14},{4,8},{6,10},{8,4},{10,6},{12,0},{14,2},{16,28},{18,... | collective-permute-start | bytes 122888 | tf_op jit(solution)/shard_map/ppermute | solution.py:22
  35.2 2.0 %collective-permute-done.5 = f32[8,1280]{1,0:T(8,128)S(1)} collective-permute-done((f32[8,1280]{1,0:T(8,128)S(1)}, f32[8,1280]{1,0:T(8,128)S(1)}, u32[]{:S(2)}, u32[]{:S(2)}) %collective-permute-start.5) | collective-permute-done | bytes 40992 | tf_op jit(solution)/shard_map/ppermute | solution.py:22
  37.2 3.8 %collective-permute-start.6 = (f32[8,1280]{1,0:T(8,128)S(1)}, f32[8,1280]{1,0:T(8,128)S(1)}, u32[]{:S(2)}, u32[]{:S(2)}) collective-permute-start(f32[8,1280]{1,0:T(8,128)S(1)} %get-tuple-element.17), channel_id=1, source_target_pairs={{0,14},{2,12},{4,10},{6,8},{8,6},{10,4},{12,2},{14,0},{16,30},{18,... | collective-permute-start | bytes 122888 | tf_op jit(solution)/shard_map/ppermute | solution.py:22
  43.0 4.1 %collective-permute-start.7 = (f32[8,1280]{1,0:T(8,128)S(1)}, f32[8,1280]{1,0:T(8,128)S(1)}, u32[]{:S(2)}, u32[]{:S(2)}) collective-permute-start(f32[8,1280]{1,0:T(8,128)S(1)} %get-tuple-element.16), channel_id=1, source_target_pairs={{0,16},{2,18},{4,20},{6,22},{8,24},{10,26},{12,28},{14,30},{16,0},... | collective-permute-start | bytes 122888 | tf_op jit(solution)/shard_map/ppermute | solution.py:22
  47.1 2.4 %collective-permute-done.7 = f32[8,1280]{1,0:T(8,128)S(1)} collective-permute-done((f32[8,1280]{1,0:T(8,128)S(1)}, f32[8,1280]{1,0:T(8,128)S(1)}, u32[]{:S(2)}, u32[]{:S(2)}) %collective-permute-start.7) | collective-permute-done | bytes 40992 | tf_op jit(solution)/shard_map/ppermute | solution.py:22
  49.5 4.2 %collective-permute-start.8 = (f32[8,1280]{1,0:T(8,128)S(1)}, f32[8,1280]{1,0:T(8,128)S(1)}, u32[]{:S(2)}, u32[]{:S(2)}) collective-permute-start(f32[8,1280]{1,0:T(8,128)S(1)} %get-tuple-element.15), channel_id=1, source_target_pairs={{0,18},{2,16},{4,22},{6,20},{8,26},{10,24},{12,30},{14,28},{16,2},... | collective-permute-start | bytes 122888 | tf_op jit(solution)/shard_map/ppermute | solution.py:22
  53.7 2.0 %collective-permute-done.8 = f32[8,1280]{1,0:T(8,128)S(1)} collective-permute-done((f32[8,1280]{1,0:T(8,128)S(1)}, f32[8,1280]{1,0:T(8,128)S(1)}, u32[]{:S(2)}, u32[]{:S(2)}) %collective-permute-start.8) | collective-permute-done | bytes 40992 | tf_op jit(solution)/shard_map/ppermute | solution.py:22
  55.7 3.5 %collective-permute-start.9 = (f32[8,1280]{1,0:T(8,128)S(1)}, f32[8,1280]{1,0:T(8,128)S(1)}, u32[]{:S(2)}, u32[]{:S(2)}) collective-permute-start(f32[8,1280]{1,0:T(8,128)S(1)} %get-tuple-element.14), channel_id=1, source_target_pairs={{0,20},{2,22},{4,16},{6,18},{8,28},{10,30},{12,24},{14,26},{16,4},... | collective-permute-start | bytes 122888 | tf_op jit(solution)/shard_map/ppermute | solution.py:22
  59.2 2.3 %collective-permute-done.9 = f32[8,1280]{1,0:T(8,128)S(1)} collective-permute-done((f32[8,1280]{1,0:T(8,128)S(1)}, f32[8,1280]{1,0:T(8,128)S(1)}, u32[]{:S(2)}, u32[]{:S(2)}) %collective-permute-start.9) | collective-permute-done | bytes 40992 | tf_op jit(solution)/shard_map/ppermute | solution.py:22
  61.5 4.4 %collective-permute-start.10 = (f32[8,1280]{1,0:T(8,128)S(1)}, f32[8,1280]{1,0:T(8,128)S(1)}, u32[]{:S(2)}, u32[]{:S(2)}) collective-permute-start(f32[8,1280]{1,0:T(8,128)S(1)} %get-tuple-element.13), channel_id=1, source_target_pairs={{0,22},{2,20},{4,18},{6,16},{8,30},{10,28},{12,26},{14,24},{16,6},... | collective-permute-start | bytes 122888 | tf_op jit(solution)/shard_map/ppermute | solution.py:22
  65.9 2.3 %collective-permute-done.10 = f32[8,1280]{1,0:T(8,128)S(1)} collective-permute-done((f32[8,1280]{1,0:T(8,128)S(1)}, f32[8,1280]{1,0:T(8,128)S(1)}, u32[]{:S(2)}, u32[]{:S(2)}) %collective-permute-start.10) | collective-permute-done | bytes 40992 | tf_op jit(solution)/shard_map/ppermute | solution.py:22
  72.4 2.1 %copy.6 = f32[2,128,1280]{2,0,1:T(2,128)} copy(f32[2,128,1280]{2,1,0:T(8,128)S(1)} %bitcast.41) | data formatting | bytes 2621440 | tf_op jit(solution)/shard_map/reshape | solution.py:148
  74.5 7.3 %all-to-all-start = ((f32[2,128,1280]{2,0,1:T(2,128)}), f32[2,128,1280]{2,0,1:T(2,128)S(1)}, u32[]{:S(2)}, u32[]{:S(2)}) async-start(f32[2,128,1280]{2,0,1:T(2,128)} %copy.6), calls=%async_computation | async-start | bytes 2621440 | tf_op jit(solution)/shard_map/all_to_all | solution.py:149
  83.2 3.0 %collective-permute-start.16 = (f32[8,5,8,3]{3,2,1,0:T(8,128)S(1)}, f32[8,5,8,3]{3,2,1,0:T(8,128)S(1)}, u32[]{:S(2)}, u32[]{:S(2)}) collective-permute-start(f32[8,5,8,3]{3,2,1,0:T(8,128)S(1)} %get-tuple-element.6), channel_id=1, source_target_pairs={{0,1},{2,3},{4,5},{6,7},{8,9},{10,11},{12,13},{14,15},{16,17},{18,... | collective-permute-start | bytes 11528 | tf_op jit(solution)/shard_map/ppermute | solution.py:34
  87.2 2.0 %fusion.12 = f32[8,5,8,512]{3,2,1,0:T(8,128)} fusion(f32[8,5,8,512]{3,2,1,0:T(8,128)S(1)} %copy-done, f32[8,5,8,3]{3,2,1,0:T(8,128)S(1)} %collective-permute-done.16, f32[8,5,8,515]{3,2,1,0:T(8,128)S(1)} %constant_dynamic-update-slice_fusion.15), kind=kLoop, calls=%fused_computation.17 | loop fusion | flops 1802240 | bytes 3280640 | tf_op jit(solution)/shard_map/div | solution.py:135
  89.2 11.8 %all-to-all-done = f32[2,128,1280]{2,0,1:T(2,128)S(1)} async-done(((f32[2,128,1280]{2,0,1:T(2,128)}), f32[2,128,1280]{2,0,1:T(2,128)S(1)}, u32[]{:S(2)}, u32[]{:S(2)}) %all-to-all-start) | async-done | bytes 1310752 | tf_op jit(solution)/shard_map/all_to_all | solution.py:149
  (78 shorter events, 21.3 us)
Async XLA Ops:
  2.4 65.9 %collective-permute-start.14 = (f32[8,1280]{1,0:T(8,128)S(1)}, f32[8,1280]{1,0:T(8,128)S(1)}, u32[]{:S(2)}, u32[]{:S(2)}) collective-permute-start(f32[8,1280]{1,0:T(8,128)S(1)} %get-tuple-element.9), channel_id=1, source_target_pairs={{0,30},{2,28},{4,26},{6,24},{8,22},{10,20},{12,18},{14,16},{16,14}... | collective-permute-start | bytes 122888 | tf_op jit(solution)/shard_map/ppermute | solution.py:22
  6.0 62.3 %collective-permute-start.13 = (f32[8,1280]{1,0:T(8,128)S(1)}, f32[8,1280]{1,0:T(8,128)S(1)}, u32[]{:S(2)}, u32[]{:S(2)}) collective-permute-start(f32[8,1280]{1,0:T(8,128)S(1)} %get-tuple-element.10), channel_id=1, source_target_pairs={{0,28},{2,30},{4,24},{6,26},{8,20},{10,22},{12,16},{14,18},{16,12}... | collective-permute-start | bytes 122888 | tf_op jit(solution)/shard_map/ppermute | solution.py:22
  6.4 61.9 %collective-permute-start.12 = (f32[8,1280]{1,0:T(8,128)S(1)}, f32[8,1280]{1,0:T(8,128)S(1)}, u32[]{:S(2)}, u32[]{:S(2)}) collective-permute-start(f32[8,1280]{1,0:T(8,128)S(1)} %get-tuple-element.11), channel_id=1, source_target_pairs={{0,26},{2,24},{4,30},{6,28},{8,18},{10,16},{12,22},{14,20},{16,10}... | collective-permute-start | bytes 122888 | tf_op jit(solution)/shard_map/ppermute | solution.py:22
  7.9 60.3 %collective-permute-start.11 = (f32[8,1280]{1,0:T(8,128)S(1)}, f32[8,1280]{1,0:T(8,128)S(1)}, u32[]{:S(2)}, u32[]{:S(2)}) collective-permute-start(f32[8,1280]{1,0:T(8,128)S(1)} %get-tuple-element.12), channel_id=1, source_target_pairs={{0,24},{2,26},{4,28},{6,30},{8,16},{10,18},{12,20},{14,22},{16,8},... | collective-permute-start | bytes 122888 | tf_op jit(solution)/shard_map/ppermute | solution.py:22
  8.4 4.0 %collective-permute-start = (f32[8,1280]{1,0:T(8,128)S(1)}, f32[8,1280]{1,0:T(8,128)S(1)}, u32[]{:S(2)}, u32[]{:S(2)}) collective-permute-start(f32[8,1280]{1,0:T(8,128)S(1)} %get-tuple-element.23), channel_id=1, source_target_pairs={{0,2},{2,0},{4,6},{6,4},{8,10},{10,8},{12,14},{14,12},{16,18},{18,... | collective-permute-start | bytes 122888 | tf_op jit(solution)/shard_map/ppermute | solution.py:22
  12.4 4.0 %collective-permute-start.1 = (f32[8,1280]{1,0:T(8,128)S(1)}, f32[8,1280]{1,0:T(8,128)S(1)}, u32[]{:S(2)}, u32[]{:S(2)}) collective-permute-start(f32[8,1280]{1,0:T(8,128)S(1)} %get-tuple-element.22), channel_id=1, source_target_pairs={{0,4},{2,6},{4,0},{6,2},{8,12},{10,14},{12,8},{14,10},{16,20},{18,... | collective-permute-start | bytes 122888 | tf_op jit(solution)/shard_map/ppermute | solution.py:22
  16.4 4.9 %collective-permute-start.2 = (f32[8,1280]{1,0:T(8,128)S(1)}, f32[8,1280]{1,0:T(8,128)S(1)}, u32[]{:S(2)}, u32[]{:S(2)}) collective-permute-start(f32[8,1280]{1,0:T(8,128)S(1)} %get-tuple-element.21), channel_id=1, source_target_pairs={{0,6},{2,4},{4,2},{6,0},{8,14},{10,12},{12,10},{14,8},{16,22},{18,... | collective-permute-start | bytes 122888 | tf_op jit(solution)/shard_map/ppermute | solution.py:22
  21.3 6.0 %collective-permute-start.3 = (f32[8,1280]{1,0:T(8,128)S(1)}, f32[8,1280]{1,0:T(8,128)S(1)}, u32[]{:S(2)}, u32[]{:S(2)}) collective-permute-start(f32[8,1280]{1,0:T(8,128)S(1)} %get-tuple-element.20), channel_id=1, source_target_pairs={{0,8},{2,10},{4,12},{6,14},{8,0},{10,2},{12,4},{14,6},{16,24},{18,... | collective-permute-start | bytes 122888 | tf_op jit(solution)/shard_map/ppermute | solution.py:22
  27.2 5.0 %collective-permute-start.4 = (f32[8,1280]{1,0:T(8,128)S(1)}, f32[8,1280]{1,0:T(8,128)S(1)}, u32[]{:S(2)}, u32[]{:S(2)}) collective-permute-start(f32[8,1280]{1,0:T(8,128)S(1)} %get-tuple-element.19), channel_id=1, source_target_pairs={{0,10},{2,8},{4,14},{6,12},{8,2},{10,0},{12,6},{14,4},{16,26},{18,... | collective-permute-start | bytes 122888 | tf_op jit(solution)/shard_map/ppermute | solution.py:22
  32.2 4.9 %collective-permute-start.5 = (f32[8,1280]{1,0:T(8,128)S(1)}, f32[8,1280]{1,0:T(8,128)S(1)}, u32[]{:S(2)}, u32[]{:S(2)}) collective-permute-start(f32[8,1280]{1,0:T(8,128)S(1)} %get-tuple-element.18), channel_id=1, source_target_pairs={{0,12},{2,14},{4,8},{6,10},{8,4},{10,6},{12,0},{14,2},{16,28},{18,... | collective-permute-start | bytes 122888 | tf_op jit(solution)/shard_map/ppermute | solution.py:22
  37.2 5.8 %collective-permute-start.6 = (f32[8,1280]{1,0:T(8,128)S(1)}, f32[8,1280]{1,0:T(8,128)S(1)}, u32[]{:S(2)}, u32[]{:S(2)}) collective-permute-start(f32[8,1280]{1,0:T(8,128)S(1)} %get-tuple-element.17), channel_id=1, source_target_pairs={{0,14},{2,12},{4,10},{6,8},{8,6},{10,4},{12,2},{14,0},{16,30},{18,... | collective-permute-start | bytes 122888 | tf_op jit(solution)/shard_map/ppermute | solution.py:22
  43.0 6.5 %collective-permute-start.7 = (f32[8,1280]{1,0:T(8,128)S(1)}, f32[8,1280]{1,0:T(8,128)S(1)}, u32[]{:S(2)}, u32[]{:S(2)}) collective-permute-start(f32[8,1280]{1,0:T(8,128)S(1)} %get-tuple-element.16), channel_id=1, source_target_pairs={{0,16},{2,18},{4,20},{6,22},{8,24},{10,26},{12,28},{14,30},{16,0},... | collective-permute-start | bytes 122888 | tf_op jit(solution)/shard_map/ppermute | solution.py:22
  49.5 6.2 %collective-permute-start.8 = (f32[8,1280]{1,0:T(8,128)S(1)}, f32[8,1280]{1,0:T(8,128)S(1)}, u32[]{:S(2)}, u32[]{:S(2)}) collective-permute-start(f32[8,1280]{1,0:T(8,128)S(1)} %get-tuple-element.15), channel_id=1, source_target_pairs={{0,18},{2,16},{4,22},{6,20},{8,26},{10,24},{12,30},{14,28},{16,2},... | collective-permute-start | bytes 122888 | tf_op jit(solution)/shard_map/ppermute | solution.py:22
  55.7 5.8 %collective-permute-start.9 = (f32[8,1280]{1,0:T(8,128)S(1)}, f32[8,1280]{1,0:T(8,128)S(1)}, u32[]{:S(2)}, u32[]{:S(2)}) collective-permute-start(f32[8,1280]{1,0:T(8,128)S(1)} %get-tuple-element.14), channel_id=1, source_target_pairs={{0,20},{2,22},{4,16},{6,18},{8,28},{10,30},{12,24},{14,26},{16,4},... | collective-permute-start | bytes 122888 | tf_op jit(solution)/shard_map/ppermute | solution.py:22
  61.5 6.7 %collective-permute-start.10 = (f32[8,1280]{1,0:T(8,128)S(1)}, f32[8,1280]{1,0:T(8,128)S(1)}, u32[]{:S(2)}, u32[]{:S(2)}) collective-permute-start(f32[8,1280]{1,0:T(8,128)S(1)} %get-tuple-element.13), channel_id=1, source_target_pairs={{0,22},{2,20},{4,18},{6,16},{8,30},{10,28},{12,26},{14,24},{16,6},... | collective-permute-start | bytes 122888 | tf_op jit(solution)/shard_map/ppermute | solution.py:22
  74.5 7.3 %copy-start = (f32[8,5,8,512]{3,2,1,0:T(8,128)S(1)}, f32[8,5,8,512]{3,2,1,0:T(8,128)}, u32[]{:S(2)}) copy-start(f32[8,5,8,512]{3,2,1,0:T(8,128)} %param.1) | copy-start | bytes 1966084
  74.5 26.5 %all-to-all-start = ((f32[2,128,1280]{2,0,1:T(2,128)}), f32[2,128,1280]{2,0,1:T(2,128)S(1)}, u32[]{:S(2)}, u32[]{:S(2)}) async-start(f32[2,128,1280]{2,0,1:T(2,128)} %copy.6), calls=%async_computation | async-start | bytes 2621440 | tf_op jit(solution)/shard_map/all_to_all | solution.py:149
  81.9 4.4 %collective-permute-start.15 = (f32[8,5,8,3]{3,2,1,0:T(8,128)S(1)}, f32[8,5,8,3]{3,2,1,0:T(8,128)S(1)}, u32[]{:S(2)}, u32[]{:S(2)}) collective-permute-start(f32[8,5,8,3]{3,2,1,0:T(8,128)S(1)} %get-tuple-element.5), channel_id=1, source_target_pairs={{1,0},{3,2},{5,4},{7,6},{9,8},{11,10},{13,12},{15,14},{17,16},{19,... | collective-permute-start | bytes 11528 | tf_op jit(solution)/shard_map/ppermute | solution.py:35
  83.2 4.1 %collective-permute-start.16 = (f32[8,5,8,3]{3,2,1,0:T(8,128)S(1)}, f32[8,5,8,3]{3,2,1,0:T(8,128)S(1)}, u32[]{:S(2)}, u32[]{:S(2)}) collective-permute-start(f32[8,5,8,3]{3,2,1,0:T(8,128)S(1)} %get-tuple-element.6), channel_id=1, source_target_pairs={{0,1},{2,3},{4,5},{6,7},{8,9},{10,11},{12,13},{14,15},{16,17},{18,... | collective-permute-start | bytes 11528 | tf_op jit(solution)/shard_map/ppermute | solution.py:34
